TPU v7x, 32 devices: a whole 2x2x4 slice. The times are simulated.
32 devices in a mesh: gx: 4 (over z), gy: 8 (over y, x, core).
Axes of the slice: x: 2, y: 2, z: 4, core: 2. Of those that a mesh axis runs over, the one named last changes fastest.
Arguments:
- leaf_up: float32 [96, 128, 456], P('gx', 'gy'), may hold values from -6 to 6
- parent_in: float32 [48, 64, 456], P('gx', 'gy'), may hold values from -6 to 6
- leaf_lists: int32 [96, 128, 40], P('gx', 'gy'), may hold values from 0 to 1, as said below
- parent_lists: int32 [48, 64, 40], P('gx', 'gy'), may hold values from 0 to 1, as said below
- up_transfer: float32 [4, 456, 456], replicated, may hold values from -0.125 to 0.125
- down_transfer: float32 [4, 456, 456], replicated, may hold values from -0.25 to 0.25
- check_inverse: float32 [456, 456], replicated, may hold values from -0.25 to 0.25
Outputs:
- leaf_down: float32 [96, 128, 456], P('gx', 'gy')
- parent_up: float32 [48, 64, 456], P('gx', 'gy')
Inputs may be any that keep to these rules, and one draw needn't show every extreme that they name: `leaf_lists`: A flag is 1 only where the box at that offset lies in the grid, its parent touches or equals the box's parent, and it holds surface points. `parent_lists`: A flag is 1 only where the parent at that offset lies in the grid, its parent touches or equals the box's parent, and it holds surface points.
All inputs are finite; a program needn't handle non-finite values.
Results may differ from a plain program's by a relative error of at most 0.0001.
Values sent between devices are 32-bit elements; how exact they have to be, the bound alone decides.
No kernel may reach another device: no remote copies, remote signals or barrier semaphores. Data moves between devices by JAX's collectives and lax.ppermute only.
A program may use at most 64 MiB of HBM per device.

v0:
```python
import functools
import math

import jax
import jax.numpy as jnp
import ml_dtypes
import numpy as np
from jax import lax
from jax.experimental import pallas as pl
from jax.experimental.pallas import tpu as pltpu
from jax.sharding import PartitionSpec as P

ORDER = 6
HALO = 4
KEPT = 14
BF16, F32 = jnp.bfloat16, jnp.float32

PARTS = (
    [(a, -2) for a in range(-1, 2)],
    [(a, 2) for a in range(-1, 2)],
    [(-2, b) for b in range(-2, 3)],
    [(2, b) for b in range(-2, 3)],
    [(3, b) for b in range(-2, 3)],
    [(-3, b) for b in range(-2, 3)],
    [(a, 3) for a in range(-3, 4)],
    [(a, -3) for a in range(-3, 4)],
)


def offset_table():
    return [(a, b) for a in range(-3, 4) for b in range(-3, 4) if max(abs(a), abs(b)) >= 2]


BASES = sorted({(abs(a), abs(b)) for a, b in offset_table()})


def surface_points():
    grid = np.linspace(-1.0, 1.0, ORDER)
    keys = [
        (i, j, k)
        for i in range(ORDER)
        for j in range(ORDER)
        for k in range(ORDER)
        if min(i, j, k) == 0 or max(i, j, k) == ORDER - 1
    ]
    return keys, np.array([[grid[i] for i in key] for key in keys])


def translation(points, dx, dy):
    r = 0.525 * (points[:, None, :] - points[None, :, :]) - np.array([dx, dy, 0.0])
    dist = np.sqrt((r * r).sum(-1))
    n = len(points)
    out = np.zeros((3, n, 3, n))
    for a in range(3):
        for b in range(3):
            out[a, :, b, :] = (float(a == b) / dist + r[..., a] * r[..., b] / dist**3) / (8 * math.pi)
    return out.reshape(3 * n, 3 * n)


def split(x):
    high = x.astype(ml_dtypes.bfloat16)
    return high, (x - high.astype(np.float64)).astype(ml_dtypes.bfloat16)


@functools.lru_cache(maxsize=None)
def operators():
    keys, points = surface_points()
    n = len(keys)
    points_of = {key: i for i, key in enumerate(keys)}
    mirror = [points_of[(i, j, ORDER - 1 - k)] for i, j, k in keys]
    mats = {o: translation(points, *o) for o in offset_table()}
    half = 3 * n // 2
    rotation = np.zeros((3 * n, 512), ml_dtypes.bfloat16)
    back = np.zeros((512, 3 * n))
    table = np.zeros((2, len(BASES), 256, 256), ml_dtypes.bfloat16)
    signs = np.ones((4, 2, 256, 256), ml_dtypes.bfloat16)
    for s, sign in enumerate((1, -1)):
        pairs = np.zeros((3 * n, half))
        firsts = []
        for a in range(3):
            flip = sign if a < 2 else -sign
            for i in range(n):
                if i < mirror[i]:
                    pairs[a * n + i, len(firsts)] = 1.0
                    pairs[a * n + mirror[i], len(firsts)] = flip
                    firsts.append(a * n + i)
        blocks = {o: 0.25 * pairs.T @ m @ pairs for o, m in mats.items()}
        gram = sum(b.T @ b for b in blocks.values())
        place = {f: i for i, f in enumerate(firsts)}
        modes, parity, weight = [], [], []
        for sx in (1, -1):
            for sy in (1, -1):
                basis = []
                for i, f in enumerate(firsts):
                    a, (kx, ky, kz) = f // n, keys[f % n]
                    if kx < ORDER // 2 and ky < ORDER // 2:
                        v = np.zeros(half)
                        for fx in range(2):
                            for fy in range(2):
                                key = (ORDER - 1 - kx if fx else kx, ORDER - 1 - ky if fy else ky, kz)
                                sign_x = (sx if a != 0 else -sx) if fx else 1
                                sign_y = (sy if a != 1 else -sy) if fy else 1
                                v[place[a * n + points_of[key]]] = 0.5 * sign_x * sign_y
                        basis.append(v)
                basis = np.array(basis).T
                w, vecs = np.linalg.eigh(basis.T @ gram @ basis)
                vecs = basis @ vecs
                vecs = vecs * np.sign(vecs[np.abs(np.round(vecs, 9)).argmax(0), np.arange(len(w))])
                modes.append(vecs)
                weight.append(w)
                parity += [(sx, sy)] * len(w)
        order = np.argsort(-np.concatenate(weight), kind="stable")
        vecs = np.concatenate(modes, axis=1)[:, order]
        parity = np.array(parity)[order]
        modes = (pairs @ vecs / math.sqrt(2.0)).astype(ml_dtypes.bfloat16)
        lows = np.concatenate([modes, modes[:, :KEPT], modes[:, :KEPT]], axis=1)
        rotation[:, 256 * s : 256 * (s + 1)] = lows
        outs, out_parity = [], []
        for sx in (1, -1):
            for sy in (1, -1):
                for f in firsts:
                    a, (kx, ky, kz) = f // n, keys[f % n]
                    if kx < ORDER // 2 and ky < ORDER // 2:
                        v = np.zeros(half)
                        for fx in range(2):
                            for fy in range(2):
                                key = (ORDER - 1 - kx if fx else kx, ORDER - 1 - ky if fy else ky, kz)
                                sign_x = (sx if a != 0 else -sx) if fx else 1
                                sign_y = (sy if a != 1 else -sy) if fy else 1
                                v[place[a * n + points_of[key]]] = sign_x * sign_y
                        outs.append(v)
                        out_parity.append((sx, sy))
        outs = np.array(outs).T
        out_parity = np.array(out_parity)
        back[256 * s : 256 * s + half] = (pairs @ outs).T
        undo = np.linalg.inv(modes[firsts].astype(np.float64))
        for q, o in enumerate(BASES):
            high, low = split(undo @ blocks[o].T @ outs * 0.25)
            table[s, q, :half, :half] = high
            table[s, q, half : half + KEPT, :half] = high[:KEPT]
            table[s, q, half + KEPT : half + 2 * KEPT, :half] = low[:KEPT]
        ins = np.concatenate([parity, parity[:KEPT], parity[:KEPT]], axis=0)
        for f in range(4):
            row = np.ones(256)
            row[: len(ins)] = (ins[:, 0] if f // 2 else 1) * (ins[:, 1] if f % 2 else 1)
            col = np.ones(256)
            col[:half] = (out_parity[:, 0] if f // 2 else 1) * (out_parity[:, 1] if f % 2 else 1)
            signs[f, s] = row[:, None] * col[None, :]
    whole = [
        table[:, BASES.index((abs(a), abs(b)))] * signs[2 * (a < 0) + (b < 0)]
        for part in PARTS
        for a, b in part
    ]
    return rotation, back.astype(ml_dtypes.bfloat16), np.concatenate(whole, axis=1)


@functools.lru_cache(maxsize=None)
def plan():
    offsets = offset_table()
    sequence = [o for part in PARTS for o in part]
    products = []
    for c, d in class_pairs():
        for place, (dx, dy) in enumerate(sequence):
            px, cs = divmod(c + dx, 2)
            py, ds = divmod(d + dy, 2)
            if abs(px) <= 1 and abs(py) <= 1:
                entry = (cs * 3 + px + 1) * 6 + ds * 3 + py + 1
                products.append((offsets.index((dx, dy)), entry, place))
    return products


def class_pairs():
    return [(c, d) for c in range(2) for d in range(2)]


def dot(a, b):
    return lax.dot_general(a, b, (((1,), (0,)), ((), ())), preferred_element_type=F32)


def dot_t(a, b):
    return lax.dot_general(a, b, (((1,), (1,)), ((), ())), preferred_element_type=F32)


def parts(x):
    high = x.astype(BF16)
    return high, (x - high.astype(F32)).astype(BF16)


def times_t(x, weight):
    xh, xl = parts(x)
    wh, wl = weight
    both = dot_t(jnp.concatenate([xh, xl], axis=0), wh)
    return both[: x.shape[0]] + (both[x.shape[0] :] + dot_t(xh, wl))


def times_exact(x, weight):
    both = dot(jnp.concatenate(parts(x), axis=0), weight)
    return both[: x.shape[0]] + both[x.shape[0] :]


def lanes(ref, *at):
    pieces = [ref[(t,) + at] for t in range(4)]
    pieces = [p.reshape(-1, 128) for p in pieces]
    return jnp.concatenate(pieces, axis=1)


def cut_tiles(dens):
    return [(t, slice(128 * t, min(128 * t + 128, dens)), slice(0, min(128, dens - 128 * t))) for t in range(4)]


def modes_of(x, rot_ref, dens):
    y = times_exact(x[:, :dens], rot_ref[...])
    lane = lax.broadcasted_iota(jnp.int32, (1, 512), 1) % 256
    half = dens // 2
    is_low = (lane >= half) & (lane < half + KEPT)
    return jnp.where(is_low, y - y.astype(BF16).astype(F32), y)


def children(ref, dens, counts, c, d):
    return jnp.concatenate(
        [
            jnp.concatenate(
                [ref[t, 2 * i + c, pl.ds(d, counts[1], stride=2), :] for i in range(counts[0])],
                axis=0,
            )
            for t in range(4)
        ],
        axis=1,
    )[:, :dens]


def own_kernel(own_ref, rot_ref, modes_ref, tiled_ref, rot_out):
    rows, cols, dens = own_ref.shape
    rot_out[...] = rot_ref[...]
    y = modes_of(own_ref[...].reshape(rows * cols, dens), rot_ref, dens)
    for t, cut, to in cut_tiles(dens):
        modes_ref[t] = y[:, 128 * t : 128 * t + 128].reshape(rows, cols, 128)
        tiled_ref[t, :, :, to] = own_ref[:, :, cut]


def pass_kernel(
    even_ref, strip0_ref, strip1_ref, own_t, own_modes_ref, rot_ref, up_ref,
    parents_ref, side_ref, pmodes, send0_ref, send1_ref,
    strip_t,
):
    rows, _, dens = strip0_ref.shape
    cols = own_modes_ref.shape[2]
    pr, pc = rows // 2, cols // 2
    boxes = pr * pc
    even_x, even_y = even_ref[0] == 1, even_ref[1] == 1
    for t, cut, to in cut_tiles(dens):
        first, second = strip0_ref[:, :, cut], strip1_ref[:, :, cut]
        strip_t[t, :, 0:HALO, to] = jnp.where(even_y, second, first)
        strip_t[t, :, HALO:, to] = jnp.where(even_y, first, second)

    parent = None
    for n, (c, d) in enumerate(class_pairs()):
        x = jnp.concatenate(
            [children(own_t, dens, (pr, pc), c, d), children(strip_t, dens, (pr, HALO), c, d)],
            axis=0,
        )
        part = times_t(x, parts(up_ref[n]))
        parent = part if parent is None else parent + part
    parents_ref[...] = parent[:boxes].reshape(pr, pc, dens)
    z = modes_of(jnp.concatenate([lanes(strip_t)[:, :dens], parent], axis=0), rot_ref, dens)
    w, p = z[: rows * 8], z[rows * 8 :]
    for t in range(4):
        cut = slice(128 * t, 128 * t + 128)
        side = w[:, cut].reshape(rows, 8, 128)
        side_ref[t] = side
        pmodes[t, 2 : 2 + pr, 4 : 4 + pc, :] = p[:boxes, cut].reshape(pr, pc, 128)
        strip = p[boxes:, cut].reshape(pr, 4, 128)
        pmodes[t, 2 : 2 + pr, 2:4, :] = strip[:, 0:2]
        pmodes[t, 2 : 2 + pr, 4 + pc : 6 + pc, :] = strip[:, 2:4]
        own = p[:boxes, cut].reshape(pr, pc, 128)
        ends = []
        for x, to in ((slice(0, 2), slice(0, 2)), (slice(rows - 2, rows), slice(pr - 2, pr))):
            ends.append(
                jnp.concatenate(
                    [own_modes_ref[t, x], jnp.concatenate([side[x, 2:6], strip[to]], axis=1), own[to]],
                    axis=1,
                )
            )
        low, high = ends
        send0_ref[t] = jnp.where(even_x, high, low)
        send1_ref[t] = jnp.where(even_x, low, high)


def near_kernel(
    own_modes_ref, side_ref, pmodes_ref, parents_ref, llist_ref, plist_ref,
    pup_ref, lut, masks_ref, edge_ref,
    modes, flat,
):
    rows, cols = own_modes_ref.shape[1:3]
    pup_ref[...] = parents_ref[...]
    pr, pc = rows // 2, cols // 2
    gr, gc = pr // 2, pc // 2
    used = pr * pc + gr * gc
    high = lut.shape[2]
    count = masks_ref.shape[0] // 4

    for t in range(4):
        modes[t, 2 : 2 + rows, 8 : 8 + cols, :] = own_modes_ref[t]
        modes[t, 2 : 2 + rows, 4:8, :] = side_ref[t, :, 0:4]
        modes[t, 2 : 2 + rows, 8 + cols : 12 + cols, :] = side_ref[t, :, 4:8]
        edge_ref[t, 0:2] = modes[t, 2:4]
        edge_ref[t, 2:4] = modes[t, rows : rows + 2]

    def gather(i, carry):
        base = 2 * (i % 3) + i // 3
        for ds in range(2):
            for py in (-1, 0, 1):
                e = i * 6 + ds * 3 + py + 1
                for t in range(4):
                    x = jnp.concatenate(
                        [
                            modes[t, base + 2 * j, pl.ds(8 + 2 * py + ds, pc, stride=2), :]
                            for j in range(pr)
                        ]
                        + [
                            pmodes_ref[t, base + 2 * j, pl.ds(4 + 2 * py + ds, gc, stride=2), :]
                            for j in range(gr)
                        ]
                        + [jnp.zeros((high - used, 128), F32)],
                        axis=0,
                    )
                    lut[e, t // 2, :, 128 * (t % 2) : 128 * (t % 2) + 128] = x.astype(BF16)
        return carry

    lax.fori_loop(0, 6, gather, 0)

    flat[0, :, :, 0 : llist_ref.shape[2]] = llist_ref[...].astype(F32)
    flat[1, 0:pr, 0:pc, 0 : plist_ref.shape[2]] = plist_ref[...].astype(F32)
    for n, (c, d) in enumerate(class_pairs()):
        flag = jnp.concatenate(
            [flat[0, 2 * i + c, pl.ds(d, pc, stride=2), :] for i in range(pr)]
            + [flat[1, 2 * i + c, pl.ds(d, gc, stride=2), :] for i in range(gr)]
            + [jnp.zeros((high - used, 128), F32)],
            axis=0,
        )
        for k in range(count):
            o = plan()[count * n + k][0]
            masks_ref[count * n + k] = jnp.broadcast_to(flag[:, o : o + 1], (high, 128)).astype(BF16)


def close_kernel(
    even_ref,
    got0_ref, got1_ref, edge_ref, pside_ref, masks, lut,
    pin_ref, back, table, down_ref, inv_ref,
    out_ref,
    edge, pmodes, fresh, acc, flat, plocal,
):
    rows, cols, dens = out_ref.shape
    pr, pc = rows // 2, cols // 2
    gr, gc = pr // 2, pc // 2
    boxes, pboxes = pr * pc, gr * gc
    high = lut.shape[2]
    count = masks.shape[0] // 4
    even = even_ref[0] == 1
    for t in range(4):
        before = jnp.where(even, got1_ref[t], got0_ref[t])
        after = jnp.where(even, got0_ref[t], got1_ref[t])
        edge[t, 2:6] = edge_ref[t]
        pmodes[t, 2 : 2 + pr] = pside_ref[t, 2 : 2 + pr]
        for x, leaf, parent in ((before, slice(0, 2), slice(0, 2)), (after, slice(6, 8), slice(2 + pr, 4 + pr))):
            edge[t, leaf, 8 : 8 + cols, :] = x[:, 0:cols]
            edge[t, leaf, 6:8, :] = x[:, cols : cols + 2]
            edge[t, leaf, 8 + cols : 10 + cols, :] = x[:, cols + 2 : cols + 4]
            pmodes[t, parent, 2:4, :] = x[:, cols + 4 : cols + 6]
            pmodes[t, parent, 4 + pc : 6 + pc, :] = x[:, cols + 6 : cols + 8]
            pmodes[t, parent, 4 : 4 + pc, :] = x[:, cols + 8 :]

    def patch(cs, carry):
        for ds in range(2):
            for py in (-1, 0, 1):
                for t in range(4):
                    at = slice(128 * (t % 2), 128 * (t % 2) + 128)
                    mine = pl.ds(8 + 2 * py + ds, pc, stride=2)
                    theirs = pl.ds(4 + 2 * py + ds, gc, stride=2)
                    e = cs * 6 + ds * 3 + py + 1
                    x = jnp.concatenate([edge[t, cs + 2 * j, mine, :] for j in range(2)], axis=0)
                    fresh[0, e, t // 2, 0:16, at] = x.astype(BF16)
                    x = jnp.concatenate([pmodes[t, cs + 2 * j, theirs, :] for j in range(4)], axis=0)
                    fresh[0, e, t // 2, 16:32, at] = x.astype(BF16)
                    x = jnp.concatenate([edge[t, 4 + cs + 2 * j, mine, :] for j in range(2)], axis=0)
                    fresh[1, e, t // 2, 0:16, at] = x.astype(BF16)
                    x = jnp.concatenate(
                        [pmodes[t, 4 + cs + 2 * j, theirs, :] for j in range(4, gr)]
                        + [jnp.zeros((high - boxes - pboxes, 128), F32)],
                        axis=0,
                    )
                    fresh[1, e, t // 2, 16:32, at] = x.astype(BF16)
        return carry

    lax.fori_loop(0, 2, patch, 0)

    runs = [(0, 3), (3, 6), (6, 11), (11, 16), (16, 21)]

    def listed(i, s):
        e = plan()[i][1]
        px = e // 6 % 3 - 1
        m = masks[i]
        if px == 0:
            x = lut[e, s]
        else:
            new = fresh[(px + 1) // 2, e // 18 * 6 + e % 6, s]
            if px < 0:
                pieces = [new[0:16], lut[e, s, 16:boxes], new[16:32], lut[e, s, boxes + 16 : high]]
            else:
                pieces = [lut[e, s, 0 : boxes - 16], new[0:16], lut[e, s, boxes : boxes + 16], new[16:32]]
            x = jnp.concatenate(pieces, axis=0)
        return jnp.concatenate([x[:, :128] * m, x[:, 128:] * m], axis=1)

    for c in range(2):

        def interact(s, carry):
            n = 2 * c
            total = jnp.zeros((2 * high, 256), F32)

            def run(first, last, s):
                at = 256 * plan()[first][2]
                x = jnp.concatenate([listed(i, s) for i in range(first, last)], axis=1)
                return x, table[s, at : at + 256 * (last - first), :]

            for a, b in runs:
                x, weight = run(n * count + a, n * count + b, s)
                y, _ = run((n + 1) * count + a, (n + 1) * count + b, s)
                total = total + dot(jnp.concatenate([x, y], axis=0), weight)
            for d in range(2):
                x, weight = run((n + d) * count + runs[-1][1], (n + d + 1) * count, s)
                acc[s, n + d] = total[high * d : high * (d + 1)] + dot(x, weight)
            return carry

        lax.fori_loop(0, 2, interact, 0)

    def densities(rows):
        pieces = [
            times_exact(
                jnp.concatenate([acc[s, n, rows] for n in range(4)], axis=0),
                back[256 * s : 256 * (s + 1)],
            )
            for s in range(2)
        ]
        return pieces[0] + pieces[1]

    pcheck = densities(slice(boxes, high))
    check = densities(slice(0, boxes))

    inverse = parts(inv_ref[...])
    for n, (c, d) in enumerate(class_pairs()):
        for t, cut, to in cut_tiles(dens):
            for j in range(gr):
                r = (high - boxes) * n + gc * j
                plocal[t, 2 * j + c, pl.ds(d, gc, stride=2), to] = pcheck[r : r + gc, cut]
    local = pin_ref[...].reshape(boxes, dens) + times_t(lanes(plocal)[:, :dens], inverse)
    x = jnp.concatenate(
        [
            check[boxes * n : boxes * (n + 1)] + times_t(local, parts(down_ref[n]))
            for n in range(4)
        ],
        axis=0,
    )
    result = times_t(x, inverse)
    for n, (c, d) in enumerate(class_pairs()):
        for t, cut, to in cut_tiles(dens):
            for j in range(pr):
                r = boxes * n + pc * j
                flat[t, 2 * j + c, pl.ds(d, pc, stride=2), to] = result[r : r + pc, cut]
    for t, cut, to in cut_tiles(dens):
        out_ref[:, :, cut] = flat[t, :, :, to]


VMEM = pl.BlockSpec(memory_space=pltpu.VMEM)
SMEM = pl.BlockSpec(memory_space=pltpu.SMEM)


def params(mib):
    return pltpu.CompilerParams(vmem_limit_bytes=mib * 1024 * 1024)


def cost(rows, tiles, reads):
    return pl.CostEstimate(flops=2 * rows * tiles * 256 * 256, bytes_accessed=reads, transcendentals=0)


def height(boxes):
    return -(-(boxes * 5 // 4) // 16) * 16


def own_step(own, rotation):
    rows, cols, _ = own.shape
    tiled = jax.ShapeDtypeStruct((4, rows, cols, 128), F32)
    return pl.pallas_call(
        own_kernel,
        out_shape=(tiled, tiled, jax.ShapeDtypeStruct(rotation.shape, BF16)),
        in_specs=[VMEM] * 2,
        out_specs=(VMEM,) * 3,
        compiler_params=params(16),
        cost_estimate=cost(rows * cols, 48, 64 * 1024 * 1024),
    )(own, rotation)


def pass_step(even, strips, tiled, own_modes, rotation, up):
    rows, cols = tiled.shape[1:3]
    dens = up.shape[1]
    pr, pc = rows // 2, cols // 2
    send = jax.ShapeDtypeStruct((4, 2, cols + pc + 8, 128), F32)
    return pl.pallas_call(
        pass_kernel,
        out_shape=(
            jax.ShapeDtypeStruct((pr, pc, dens), F32),
            jax.ShapeDtypeStruct((4, rows, 2 * HALO, 128), F32),
            jax.ShapeDtypeStruct((4, pr + 4, pc + 8, 128), F32),
            send,
            send,
        ),
        in_specs=[SMEM] + [VMEM] * 6,
        out_specs=(VMEM,) * 5,
        scratch_shapes=[pltpu.VMEM((4, rows, 2 * HALO, 128), F32)],
        compiler_params=params(16),
        cost_estimate=cost(rows * cols, 32, up.size * 4),
    )(even, *strips, tiled, own_modes, rotation, up)


def near_step(own_modes, side, pmodes, parents, llist, plist):
    rows, cols, _ = llist.shape
    high = height(rows * cols // 4)
    return pl.pallas_call(
        near_kernel,
        out_shape=(
            jax.ShapeDtypeStruct(parents.shape, F32),
            jax.ShapeDtypeStruct((36, 2, high, 256), BF16),
            jax.ShapeDtypeStruct((len(plan()), high, 128), BF16),
            jax.ShapeDtypeStruct((4, 4, cols + 16, 128), F32),
        ),
        in_specs=[VMEM] * 6,
        out_specs=(VMEM,) * 4,
        scratch_shapes=[
            pltpu.VMEM((4, rows + 4, cols + 16, 128), F32),
            pltpu.VMEM((2, rows, cols, 128), F32),
        ],
        compiler_params=params(16),
        cost_estimate=cost(rows * cols, 48, 16 * 1024 * 1024),
    )(own_modes, side, pmodes, parents, llist, plist)


def close_step(even, ends, edge, pmodes, masks, lut, pin, back, table, down, inv, shape):
    rows, cols, dens = shape
    pr, pc = rows // 2, cols // 2
    high = height(pr * pc)
    return pl.pallas_call(
        close_kernel,
        out_shape=jax.ShapeDtypeStruct(shape, F32),
        in_specs=[SMEM] + [VMEM] * 11,
        out_specs=VMEM,
        scratch_shapes=[
            pltpu.VMEM((4, 8, cols + 16, 128), F32),
            pltpu.VMEM((4, pr + 4, pc + 8, 128), F32),
            pltpu.VMEM((2, 12, 2, 32, 256), BF16),
            pltpu.VMEM((2, 4, high, 256), F32),
            pltpu.VMEM((4, rows, cols, 128), F32),
            pltpu.VMEM((4, pr, pc, 128), F32),
        ],
        compiler_params=params(24),
        cost_estimate=cost(rows * cols, 150, table.size * 2),
    )(
        even, *ends, edge, pmodes, masks, lut, pin, back, table, down, inv,
    )


def swapped(strips, axis, odd_first):
    peers = lax.axis_size(axis)
    got = [None, None]
    for kind in (1, 0) if odd_first else (0, 1):
        pairs = [(i, i + 1) for i in range(kind, peers - 1, 2)]
        got[kind] = lax.ppermute(strips[kind], axis, pairs + [(j, i) for i, j in pairs])
    return got


def local(leaf_up, parent_in, leaf_lists, parent_lists, up_transfer, down_transfer, check_inverse):
    cols = leaf_up.shape[1]
    even = [lax.axis_index(axis) % 2 == 0 for axis in ("gx", "gy")]
    flag = jnp.stack(even).astype(jnp.int32)
    rotation, back, table = (jnp.asarray(x) for x in operators())
    low, high = leaf_up[:, :HALO], leaf_up[:, cols - HALO :]
    strips = (jnp.where(even[1], high, low), jnp.where(even[1], low, high))
    strips = swapped(strips, "gy", True)
    own_modes, tiled, rotation = own_step(leaf_up, rotation)
    parents, side, pmodes, *sends = pass_step(flag, strips, tiled, own_modes, rotation, up_transfer)
    ends = swapped(sends, "gx", False)
    parent_up, lut, masks, edge = near_step(
        own_modes, side, pmodes, parents, leaf_lists, parent_lists
    )
    leaf_down = close_step(
        flag, ends, edge, pmodes, masks, lut, parent_in, back, table,
        down_transfer, check_inverse, leaf_up.shape,
    )
    return leaf_down, parent_up


def solution(mesh):
    block = P("gx", "gy", None)
    return jax.shard_map(
        local,
        mesh=mesh,
        in_specs=(block,) * 4 + (P(),) * 3,
        out_specs=(block, block),
        check_vma=False,
    )
```

profile of v0, /device:TPU:19, one launch (start us, length us, event | category | flops | bytes accessed | tf_op | source)
XLA Modules:
  0.0 31.7 jit_solution(9281551680261750774)
XLA Ops:
  0.6 1.2 %slice_select_fusion = (f32[24,4,456]{2,1,0:T(4,128)S(1)}, f32[24,4,456]{2,1,0:T(4,128)S(1)}) fusion(f32[24,16,456]{2,1,0:T(8,128)} %own_ref.1, pred[]{:T(512)} %eq.10), kind=kLoop, calls=%fused_computation | loop fusion | flops 87552 | bytes 700417 | tf_op jit(solution)/shard_map/jit(_where)/select_n | solution.py:585
  1.8 3.7 %collective-permute-start.1 = (f32[24,4,456]{2,1,0:T(4,128)S(1)}, f32[24,4,456]{2,1,0:T(4,128)S(1)}, u32[]{:S(2)}, u32[]{:S(2)}) collective-permute-start(f32[24,4,456]{2,1,0:T(4,128)S(1)} %get-tuple-element.26), channel_id=1, source_target_pairs={{1,2},{3,4},{5,6},{2,1},{4,3},{6,5},{9,10},{11,12},{13,14},{10,9},... | collective-permute-start | bytes 525320 | tf_op jit(solution)/shard_map/ppermute | solution.py:575
  5.5 0.1 collective-permute-start
  5.6 0.1 add_convert_fusion.even_ref
  5.7 0.0 copy-start.1
  5.7 1.1 %copy-done.1 = f32[24,16,456]{2,1,0:T(8,128)S(1)} copy-done((f32[24,16,456]{2,1,0:T(8,128)S(1)}, f32[24,16,456]{2,1,0:T(8,128)}, u32[]{:S(2)}) %copy-start.1) | copy-done | bytes 700440
  6.8 0.0 copy-start.9
  6.8 1.0 %copy-done.9 = bf16[456,512]{1,0:T(8,128)(2,1)S(1)} copy-done((bf16[456,512]{1,0:T(8,128)(2,1)S(1)}, bf16[456,512]{1,0:T(8,128)(2,1)}, u32[]{:S(2)}) %copy-start.9) | copy-done | bytes 466968
  7.9 0.0 copy-start
  7.9 0.0 copy-start.7
  7.9 0.6 %shard_map.113 = (f32[4,24,16,128]{3,2,1,0:T(8,128)S(1)}, f32[4,24,16,128]{3,2,1,0:T(8,128)S(1)}, bf16[456,512]{1,0:T(8,128)(2,1)S(1)}) custom-call(f32[24,16,456]{2,1,0:T(8,128)S(1)} %copy-done.1, bf16[456,512]{1,0:T(8,128)(2,1)S(1)} %copy-done.9), custom_call_target="tpu_custom_call" | custom-call | flops 2415919104 | bytes 67108864 | tf_op jit(solution)/shard_map/pallas_call | solution.py:492
  8.5 0.0 copy-start.4
  8.5 0.0 copy-start.6
  8.5 3.3 %collective-permute-done.1.strip1_ref = f32[24,4,456]{2,1,0:T(4,128)S(1)} collective-permute-done((f32[24,4,456]{2,1,0:T(4,128)S(1)}, f32[24,4,456]{2,1,0:T(4,128)S(1)}, u32[]{:S(2)}, u32[]{:S(2)}) %collective-permute-start.1) | collective-permute-done | bytes 175136 | tf_op jit(solution)/shard_map/ppermute | solution.py:575
  11.8 0.0 collective-permute-done.strip0_ref
  11.8 0.0 copy-done
  11.8 2.5 %shard_map.114 = (f32[12,8,456]{2,1,0:T(8,128)S(1)}, f32[4,24,8,128]{3,2,1,0:T(8,128)S(1)}, f32[4,16,16,128]{3,2,1,0:T(8,128)S(1)}, f32[4,2,32,128]{3,2,1,0:T(8,128)S(1)}, f32[4,2,32,128]{3,2,1,0:T(8,128)S(1)}) custom-call(s32[2]{0:T(128)S(1)} %add_convert_fusion.even_ref, f32[24,4,456]{2,1,0:T(4,128)S(1)} %collective-permute-done.strip0_ref, ...), custom_call_target="tpu_custom_call" | custom-call | flops 1610612736 | bytes 3326976 | tf_op jit(solution)/shard_map/pallas_call | solution.py:507
  14.3 1.4 %collective-permute-start.2 = (f32[4,2,32,128]{3,2,1,0:T(8,128)S(1)}, f32[4,2,32,128]{3,2,1,0:T(8,128)S(1)}, u32[]{:S(2)}, u32[]{:S(2)}) collective-permute-start(f32[4,2,32,128]{3,2,1,0:T(8,128)S(1)} %get-tuple-element.17), channel_id=1, source_target_pairs={{0,8},{16,24},{8,0},{24,16},{1,9},{17,25},{9,1},{25,17},{2,10},{18... | collective-permute-start | bytes 393224 | tf_op jit(solution)/shard_map/ppermute | solution.py:575
  15.7 1.9 %collective-permute-start.3 = (f32[4,2,32,128]{3,2,1,0:T(8,128)S(1)}, f32[4,2,32,128]{3,2,1,0:T(8,128)S(1)}, u32[]{:S(2)}, u32[]{:S(2)}) collective-permute-start(f32[4,2,32,128]{3,2,1,0:T(8,128)S(1)} %get-tuple-element.18), channel_id=1, source_target_pairs={{8,16},{16,8},{9,17},{17,9},{10,18},{18,10},{11,19},{19,11},{12,20... | collective-permute-start | bytes 393224 | tf_op jit(solution)/shard_map/ppermute | solution.py:575
  17.6 0.0 copy-done.4
  17.6 0.0 copy-done.6
  17.6 0.0 copy-start.2
  17.6 0.0 copy-start.3
  17.7 0.0 copy-start.5
  17.7 0.0 copy-start.8
  17.7 2.8 %shard_map.115 = (f32[12,8,456]{2,1,0:T(8,128)}, bf16[36,2,128,256]{3,2,1,0:T(8,128)(2,1)S(1)}, bf16[108,128,128]{2,1,0:T(8,128)(2,1)S(1)}, f32[4,4,32,128]{3,2,1,0:T(8,128)S(1)}) custom-call(f32[4,24,16,128]{3,2,1,0:T(8,128)S(1)} %get-tuple-element.15.own_modes_ref, f32[4,24,8,128]{3,2,1,0:T(8,128)S(1)} %get-tuple-element.19.side_ref, ...), custom_call_target="tpu_custom_call" | custom-call | flops 2415919104 | bytes 16777216 | tf_op jit(solution)/shard_map/pallas_call | solution.py:527
  20.4 0.0 collective-permute-done.2.got0_ref
  20.4 1.8 %collective-permute-done.3.got1_ref = f32[4,2,32,128]{3,2,1,0:T(8,128)S(1)} collective-permute-done((f32[4,2,32,128]{3,2,1,0:T(8,128)S(1)}, f32[4,2,32,128]{3,2,1,0:T(8,128)S(1)}, u32[]{:S(2)}, u32[]{:S(2)}) %collective-permute-start.3) | collective-permute-done | bytes 131104 | tf_op jit(solution)/shard_map/ppermute | solution.py:575
  22.2 0.0 copy-done.7
  22.2 0.0 copy-done.2
  22.3 0.0 copy-done.3
  22.3 0.0 copy-done.5
  22.3 0.0 copy-done.8
  22.3 9.5 %shard_map.116 = f32[24,16,456]{2,1,0:T(8,128)} custom-call(s32[2]{0:T(128)S(1)} %add_convert_fusion.even_ref, f32[4,2,32,128]{3,2,1,0:T(8,128)S(1)} %collective-permute-done.2.got0_ref, f32[4,2,32,128]{3,2,1,0:T(8,128)S(1)} %collective-permute-done.3.got1_ref, f32[4,4,32,128]{3,2,1,0:T(8,128)S(1)} %get-tuple-element.22.edge_ref, ...), custom_call_target="tpu_custom_call" | custom-call | flops 7549747200 | bytes 10485760 | tf_op jit(solution)/shard_map/pallas_call | solution.py:550
Async XLA Ops:
  1.8 10.0 %collective-permute-start.1 = (f32[24,4,456]{2,1,0:T(4,128)S(1)}, f32[24,4,456]{2,1,0:T(4,128)S(1)}, u32[]{:S(2)}, u32[]{:S(2)}) collective-permute-start(f32[24,4,456]{2,1,0:T(4,128)S(1)} %get-tuple-element.26), channel_id=1, source_target_pairs={{1,2},{3,4},{5,6},{2,1},{4,3},{6,5},{9,10},{11,12},{13,14},{10,9},... | collective-permute-start | bytes 525320 | tf_op jit(solution)/shard_map/ppermute | solution.py:575
  5.5 6.3 %collective-permute-start = (f32[24,4,456]{2,1,0:T(4,128)S(1)}, f32[24,4,456]{2,1,0:T(4,128)S(1)}, u32[]{:S(2)}, u32[]{:S(2)}) collective-permute-start(f32[24,4,456]{2,1,0:T(4,128)S(1)} %get-tuple-element.27), channel_id=1, source_target_pairs={{0,1},{2,3},{4,5},{6,7},{1,0},{3,2},{5,4},{7,6},{8,9},{10,11},{12,... | collective-permute-start | bytes 525320 | tf_op jit(solution)/shard_map/ppermute | solution.py:575
  5.7 1.1 %copy-start.1 = (f32[24,16,456]{2,1,0:T(8,128)S(1)}, f32[24,16,456]{2,1,0:T(8,128)}, u32[]{:S(2)}) copy-start(f32[24,16,456]{2,1,0:T(8,128)} %own_ref.1) | copy-start | bytes 2101252
  6.8 1.0 %copy-start.9 = (bf16[456,512]{1,0:T(8,128)(2,1)S(1)}, bf16[456,512]{1,0:T(8,128)(2,1)}, u32[]{:S(2)}) copy-start(bf16[456,512]{1,0:T(8,128)(2,1)} %constant.32.clone.rot_ref) | copy-start | bytes 1400836
  7.9 3.9 %copy-start = (f32[4,456,456]{2,1,0:T(8,128)S(1)}, f32[4,456,456]{2,1,0:T(8,128)}, u32[]{:S(2)}) copy-start(f32[4,456,456]{2,1,0:T(8,128)} %up_ref.1) | copy-start | bytes 9980932
  7.9 14.4 %copy-start.7 = (bf16[2,10240,256]{2,1,0:T(8,128)(2,1)S(1)}, bf16[2,10240,256]{2,1,0:T(8,128)(2,1)}, u32[]{:S(2)}) copy-start(bf16[2,10240,256]{2,1,0:T(8,128)(2,1)} %constant.34.clone.table) | copy-start | bytes 31457284
  8.5 9.1 %copy-start.4 = (s32[24,16,40]{2,1,0:T(8,128)S(1)}, s32[24,16,40]{2,1,0:T(8,128)}, u32[]{:S(2)}) copy-start(s32[24,16,40]{2,1,0:T(8,128)} %llist_ref.1) | copy-start | bytes 184324
  8.5 9.1 %copy-start.6 = (s32[12,8,40]{2,1,0:T(8,128)S(1)}, s32[12,8,40]{2,1,0:T(8,128)}, u32[]{:S(2)}) copy-start(s32[12,8,40]{2,1,0:T(8,128)} %plist_ref.1) | copy-start | bytes 46084
  14.3 6.1 %collective-permute-start.2 = (f32[4,2,32,128]{3,2,1,0:T(8,128)S(1)}, f32[4,2,32,128]{3,2,1,0:T(8,128)S(1)}, u32[]{:S(2)}, u32[]{:S(2)}) collective-permute-start(f32[4,2,32,128]{3,2,1,0:T(8,128)S(1)} %get-tuple-element.17), channel_id=1, source_target_pairs={{0,8},{16,24},{8,0},{24,16},{1,9},{17,25},{9,1},{25,17},{2,10},{18... | collective-permute-start | bytes 393224 | tf_op jit(solution)/shard_map/ppermute | solution.py:575
  15.7 6.6 %collective-permute-start.3 = (f32[4,2,32,128]{3,2,1,0:T(8,128)S(1)}, f32[4,2,32,128]{3,2,1,0:T(8,128)S(1)}, u32[]{:S(2)}, u32[]{:S(2)}) collective-permute-start(f32[4,2,32,128]{3,2,1,0:T(8,128)S(1)} %get-tuple-element.18), channel_id=1, source_target_pairs={{8,16},{16,8},{9,17},{17,9},{10,18},{18,10},{11,19},{19,11},{12,20... | collective-permute-start | bytes 393224 | tf_op jit(solution)/shard_map/ppermute | solution.py:575
  17.6 4.6 %copy-start.2 = (f32[4,456,456]{2,1,0:T(8,128)S(1)}, f32[4,456,456]{2,1,0:T(8,128)}, u32[]{:S(2)}) copy-start(f32[4,456,456]{2,1,0:T(8,128)} %down_ref.1) | copy-start | bytes 9980932
  17.6 4.6 %copy-start.3 = (f32[456,456]{1,0:T(8,128)S(1)}, f32[456,456]{1,0:T(8,128)}, u32[]{:S(2)}) copy-start(f32[456,456]{1,0:T(8,128)} %inv_ref.1) | copy-start | bytes 2495236
  17.7 4.6 %copy-start.5 = (f32[12,8,456]{2,1,0:T(8,128)S(1)}, f32[12,8,456]{2,1,0:T(8,128)}, u32[]{:S(2)}) copy-start(f32[12,8,456]{2,1,0:T(8,128)} %pin_ref.1) | copy-start | bytes 525316
  17.7 4.6 %copy-start.8 = (bf16[512,456]{1,0:T(8,128)(2,1)S(1)}, bf16[512,456]{1,0:T(8,128)(2,1)}, u32[]{:S(2)}) copy-start(bf16[512,456]{1,0:T(8,128)(2,1)} %constant.33.clone.back) | copy-start | bytes 1400836
where the time goes:
time: 32 us; the launch traced here: 31.7 us
  Pallas kernels  15.3 us (48%)
  starting transfers between devices  7.02 us (22%)
  waiting for transfers between devices  5.12 us (16%)
  local copies, waits for them, and re-layouts  2.2 us (7%)
  other arithmetic  1.27 us (4%)
  between operations  0.79 us (2%)
    pallas_call x1, Pallas kernels, close_step(): pl.pallas_call(close_kernel, out_shape=jax.ShapeDtypeStruct(shape, F32),...  9.47 us
    ppermute x4, starting transfers between devices, swapped(): lax.ppermute(strips[kind], axis, pairs + [(j, i) for i, j in pairs])  7.02 us
    ppermute x4, waiting for transfers between devices, swapped(): lax.ppermute(strips[kind], axis, pairs + [(j, i) for i, j in pairs])  5.12 us
    pallas_call x1, Pallas kernels, near_step(): pl.pallas_call(near_kernel, out_shape=(jax.ShapeDtypeStruct(parents.shape...  2.76 us
    pallas_call x1, Pallas kernels, pass_step(): pl.pallas_call(pass_kernel, out_shape=(jax.ShapeDtypeStruct((pr, pc, dens...  2.52 us
    unnamed x20, local copies, waits for them, and re-layouts  2.2 us
    select_n x1, other arithmetic, local(): strips = (jnp.where(even[1], high, low), jnp.where(even[1], low, high))  1.2 us
  transfers between devices with their start and end apart: 4, of which 2 were waited for; matrix products, arithmetic and copies ran while one was open for 0% of the time, Pallas kernels for 11%

commit v1 on v0

--- a/solution.py
+++ b/solution.py
@@ -431,7 +431,8 @@
                 acc[s, n + d] = total[high * d : high * (d + 1)] + dot(x, weight)
             return carry
 
-        lax.fori_loop(0, 2, interact, 0)
+        for s in range(2):
+            interact(s, 0)
 
     def densities(rows):
         pieces = [

time: 32 us -> 31.4 us (0.981)
  Pallas kernels: 15.3 us -> 14.7 us
    pallas_call x1, Pallas kernels: 9.47 us -> 8.83 us  [close_step(): pl.pallas_call(close_kernel, out_shape=jax.ShapeDtypeStruct(shape, F32),...]
where the time goes in v1:
time: 31.4 us; the launch traced here: 31.1 us
  Pallas kernels  14.7 us (47%)
  starting transfers between devices  7.02 us (22%)
  waiting for transfers between devices  5.12 us (16%)
  local copies, waits for them, and re-layouts  2.2 us (7%)
  other arithmetic  1.27 us (4%)
  between operations  0.79 us (3%)
    pallas_call x1, Pallas kernels, close_step(): pl.pallas_call(close_kernel, out_shape=jax.ShapeDtypeStruct(shape, F32),...  8.83 us
    ppermute x4, starting transfers between devices, swapped(): lax.ppermute(strips[kind], axis, pairs + [(j, i) for i, j in pairs])  7.02 us
    ppermute x4, waiting for transfers between devices, swapped(): lax.ppermute(strips[kind], axis, pairs + [(j, i) for i, j in pairs])  5.12 us
    pallas_call x1, Pallas kernels, near_step(): pl.pallas_call(near_kernel, out_shape=(jax.ShapeDtypeStruct(parents.shape...  2.76 us
    pallas_call x1, Pallas kernels, pass_step(): pl.pallas_call(pass_kernel, out_shape=(jax.ShapeDtypeStruct((pr, pc, dens...  2.52 us
    unnamed x20, local copies, waits for them, and re-layouts  2.2 us
    select_n x1, other arithmetic, local(): strips = (jnp.where(even[1], high, low), jnp.where(even[1], low, high))  1.2 us
  transfers between devices with their start and end apart: 4, of which 2 were waited for; matrix products, arithmetic and copies ran while one was open for 0% of the time, Pallas kernels for 11%

profile of v1, /device:TPU:19, one launch (start us, length us, event | category | flops | bytes accessed | tf_op | source)
XLA Modules:
  0.0 31.1 jit_solution(8345470704414775849)
XLA Ops:
  0.6 1.2 %slice_select_fusion = (f32[24,4,456]{2,1,0:T(4,128)S(1)}, f32[24,4,456]{2,1,0:T(4,128)S(1)}) fusion(f32[24,16,456]{2,1,0:T(8,128)} %own_ref.1, pred[]{:T(512)} %eq.10), kind=kLoop, calls=%fused_computation | loop fusion | flops 87552 | bytes 700417 | tf_op jit(solution)/shard_map/jit(_where)/select_n | solution.py:586
  1.8 3.7 %collective-permute-start.1 = (f32[24,4,456]{2,1,0:T(4,128)S(1)}, f32[24,4,456]{2,1,0:T(4,128)S(1)}, u32[]{:S(2)}, u32[]{:S(2)}) collective-permute-start(f32[24,4,456]{2,1,0:T(4,128)S(1)} %get-tuple-element.26), channel_id=1, source_target_pairs={{1,2},{3,4},{5,6},{2,1},{4,3},{6,5},{9,10},{11,12},{13,14},{10,9},... | collective-permute-start | bytes 525320 | tf_op jit(solution)/shard_map/ppermute | solution.py:576
  5.5 0.1 collective-permute-start
  5.6 0.1 add_convert_fusion.even_ref
  5.7 0.0 copy-start.1
  5.7 1.1 %copy-done.1 = f32[24,16,456]{2,1,0:T(8,128)S(1)} copy-done((f32[24,16,456]{2,1,0:T(8,128)S(1)}, f32[24,16,456]{2,1,0:T(8,128)}, u32[]{:S(2)}) %copy-start.1) | copy-done | bytes 700440
  6.8 0.0 copy-start.9
  6.8 1.0 %copy-done.9 = bf16[456,512]{1,0:T(8,128)(2,1)S(1)} copy-done((bf16[456,512]{1,0:T(8,128)(2,1)S(1)}, bf16[456,512]{1,0:T(8,128)(2,1)}, u32[]{:S(2)}) %copy-start.9) | copy-done | bytes 466968
  7.9 0.0 copy-start
  7.9 0.0 copy-start.7
  7.9 0.6 %shard_map.113 = (f32[4,24,16,128]{3,2,1,0:T(8,128)S(1)}, f32[4,24,16,128]{3,2,1,0:T(8,128)S(1)}, bf16[456,512]{1,0:T(8,128)(2,1)S(1)}) custom-call(f32[24,16,456]{2,1,0:T(8,128)S(1)} %copy-done.1, bf16[456,512]{1,0:T(8,128)(2,1)S(1)} %copy-done.9), custom_call_target="tpu_custom_call" | custom-call | flops 2415919104 | bytes 67108864 | tf_op jit(solution)/shard_map/pallas_call | solution.py:493
  8.5 0.0 copy-start.4
  8.5 0.0 copy-start.6
  8.5 3.3 %collective-permute-done.1.strip1_ref = f32[24,4,456]{2,1,0:T(4,128)S(1)} collective-permute-done((f32[24,4,456]{2,1,0:T(4,128)S(1)}, f32[24,4,456]{2,1,0:T(4,128)S(1)}, u32[]{:S(2)}, u32[]{:S(2)}) %collective-permute-start.1) | collective-permute-done | bytes 175136 | tf_op jit(solution)/shard_map/ppermute | solution.py:576
  11.8 0.0 collective-permute-done.strip0_ref
  11.8 0.0 copy-done
  11.8 2.5 %shard_map.114 = (f32[12,8,456]{2,1,0:T(8,128)S(1)}, f32[4,24,8,128]{3,2,1,0:T(8,128)S(1)}, f32[4,16,16,128]{3,2,1,0:T(8,128)S(1)}, f32[4,2,32,128]{3,2,1,0:T(8,128)S(1)}, f32[4,2,32,128]{3,2,1,0:T(8,128)S(1)}) custom-call(s32[2]{0:T(128)S(1)} %add_convert_fusion.even_ref, f32[24,4,456]{2,1,0:T(4,128)S(1)} %collective-permute-done.strip0_ref, ...), custom_call_target="tpu_custom_call" | custom-call | flops 1610612736 | bytes 3326976 | tf_op jit(solution)/shard_map/pallas_call | solution.py:508
  14.3 1.4 %collective-permute-start.2 = (f32[4,2,32,128]{3,2,1,0:T(8,128)S(1)}, f32[4,2,32,128]{3,2,1,0:T(8,128)S(1)}, u32[]{:S(2)}, u32[]{:S(2)}) collective-permute-start(f32[4,2,32,128]{3,2,1,0:T(8,128)S(1)} %get-tuple-element.17), channel_id=1, source_target_pairs={{0,8},{16,24},{8,0},{24,16},{1,9},{17,25},{9,1},{25,17},{2,10},{18... | collective-permute-start | bytes 393224 | tf_op jit(solution)/shard_map/ppermute | solution.py:576
  15.7 1.9 %collective-permute-start.3 = (f32[4,2,32,128]{3,2,1,0:T(8,128)S(1)}, f32[4,2,32,128]{3,2,1,0:T(8,128)S(1)}, u32[]{:S(2)}, u32[]{:S(2)}) collective-permute-start(f32[4,2,32,128]{3,2,1,0:T(8,128)S(1)} %get-tuple-element.18), channel_id=1, source_target_pairs={{8,16},{16,8},{9,17},{17,9},{10,18},{18,10},{11,19},{19,11},{12,20... | collective-permute-start | bytes 393224 | tf_op jit(solution)/shard_map/ppermute | solution.py:576
  17.6 0.0 copy-done.4
  17.6 0.0 copy-done.6
  17.6 0.0 copy-start.2
  17.6 0.0 copy-start.3
  17.7 0.0 copy-start.5
  17.7 0.0 copy-start.8
  17.7 2.8 %shard_map.115 = (f32[12,8,456]{2,1,0:T(8,128)}, bf16[36,2,128,256]{3,2,1,0:T(8,128)(2,1)S(1)}, bf16[108,128,128]{2,1,0:T(8,128)(2,1)S(1)}, f32[4,4,32,128]{3,2,1,0:T(8,128)S(1)}) custom-call(f32[4,24,16,128]{3,2,1,0:T(8,128)S(1)} %get-tuple-element.15.own_modes_ref, f32[4,24,8,128]{3,2,1,0:T(8,128)S(1)} %get-tuple-element.19.side_ref, ...), custom_call_target="tpu_custom_call" | custom-call | flops 2415919104 | bytes 16777216 | tf_op jit(solution)/shard_map/pallas_call | solution.py:528
  20.4 0.0 collective-permute-done.2.got0_ref
  20.4 1.8 %collective-permute-done.3.got1_ref = f32[4,2,32,128]{3,2,1,0:T(8,128)S(1)} collective-permute-done((f32[4,2,32,128]{3,2,1,0:T(8,128)S(1)}, f32[4,2,32,128]{3,2,1,0:T(8,128)S(1)}, u32[]{:S(2)}, u32[]{:S(2)}) %collective-permute-start.3) | collective-permute-done | bytes 131104 | tf_op jit(solution)/shard_map/ppermute | solution.py:576
  22.2 0.0 copy-done.7
  22.2 0.0 copy-done.2
  22.3 0.0 copy-done.3
  22.3 0.0 copy-done.5
  22.3 0.0 copy-done.8
  22.3 8.8 %shard_map.116 = f32[24,16,456]{2,1,0:T(8,128)} custom-call(s32[2]{0:T(128)S(1)} %add_convert_fusion.even_ref, f32[4,2,32,128]{3,2,1,0:T(8,128)S(1)} %collective-permute-done.2.got0_ref, f32[4,2,32,128]{3,2,1,0:T(8,128)S(1)} %collective-permute-done.3.got1_ref, f32[4,4,32,128]{3,2,1,0:T(8,128)S(1)} %get-tuple-element.22.edge_ref, ...), custom_call_target="tpu_custom_call" | custom-call | flops 7549747200 | bytes 10485760 | tf_op jit(solution)/shard_map/pallas_call | solution.py:551
Async XLA Ops:
  1.8 10.0 %collective-permute-start.1 = (f32[24,4,456]{2,1,0:T(4,128)S(1)}, f32[24,4,456]{2,1,0:T(4,128)S(1)}, u32[]{:S(2)}, u32[]{:S(2)}) collective-permute-start(f32[24,4,456]{2,1,0:T(4,128)S(1)} %get-tuple-element.26), channel_id=1, source_target_pairs={{1,2},{3,4},{5,6},{2,1},{4,3},{6,5},{9,10},{11,12},{13,14},{10,9},... | collective-permute-start | bytes 525320 | tf_op jit(solution)/shard_map/ppermute | solution.py:576
  5.5 6.3 %collective-permute-start = (f32[24,4,456]{2,1,0:T(4,128)S(1)}, f32[24,4,456]{2,1,0:T(4,128)S(1)}, u32[]{:S(2)}, u32[]{:S(2)}) collective-permute-start(f32[24,4,456]{2,1,0:T(4,128)S(1)} %get-tuple-element.27), channel_id=1, source_target_pairs={{0,1},{2,3},{4,5},{6,7},{1,0},{3,2},{5,4},{7,6},{8,9},{10,11},{12,... | collective-permute-start | bytes 525320 | tf_op jit(solution)/shard_map/ppermute | solution.py:576
  5.7 1.1 %copy-start.1 = (f32[24,16,456]{2,1,0:T(8,128)S(1)}, f32[24,16,456]{2,1,0:T(8,128)}, u32[]{:S(2)}) copy-start(f32[24,16,456]{2,1,0:T(8,128)} %own_ref.1) | copy-start | bytes 2101252
  6.8 1.0 %copy-start.9 = (bf16[456,512]{1,0:T(8,128)(2,1)S(1)}, bf16[456,512]{1,0:T(8,128)(2,1)}, u32[]{:S(2)}) copy-start(bf16[456,512]{1,0:T(8,128)(2,1)} %constant.32.clone.rot_ref) | copy-start | bytes 1400836
  7.9 3.9 %copy-start = (f32[4,456,456]{2,1,0:T(8,128)S(1)}, f32[4,456,456]{2,1,0:T(8,128)}, u32[]{:S(2)}) copy-start(f32[4,456,456]{2,1,0:T(8,128)} %up_ref.1) | copy-start | bytes 9980932
  7.9 14.4 %copy-start.7 = (bf16[2,10240,256]{2,1,0:T(8,128)(2,1)S(1)}, bf16[2,10240,256]{2,1,0:T(8,128)(2,1)}, u32[]{:S(2)}) copy-start(bf16[2,10240,256]{2,1,0:T(8,128)(2,1)} %constant.34.clone.table) | copy-start | bytes 31457284
  8.5 9.1 %copy-start.4 = (s32[24,16,40]{2,1,0:T(8,128)S(1)}, s32[24,16,40]{2,1,0:T(8,128)}, u32[]{:S(2)}) copy-start(s32[24,16,40]{2,1,0:T(8,128)} %llist_ref.1) | copy-start | bytes 184324
  8.5 9.1 %copy-start.6 = (s32[12,8,40]{2,1,0:T(8,128)S(1)}, s32[12,8,40]{2,1,0:T(8,128)}, u32[]{:S(2)}) copy-start(s32[12,8,40]{2,1,0:T(8,128)} %plist_ref.1) | copy-start | bytes 46084
  14.3 6.1 %collective-permute-start.2 = (f32[4,2,32,128]{3,2,1,0:T(8,128)S(1)}, f32[4,2,32,128]{3,2,1,0:T(8,128)S(1)}, u32[]{:S(2)}, u32[]{:S(2)}) collective-permute-start(f32[4,2,32,128]{3,2,1,0:T(8,128)S(1)} %get-tuple-element.17), channel_id=1, source_target_pairs={{0,8},{16,24},{8,0},{24,16},{1,9},{17,25},{9,1},{25,17},{2,10},{18... | collective-permute-start | bytes 393224 | tf_op jit(solution)/shard_map/ppermute | solution.py:576
  15.7 6.6 %collective-permute-start.3 = (f32[4,2,32,128]{3,2,1,0:T(8,128)S(1)}, f32[4,2,32,128]{3,2,1,0:T(8,128)S(1)}, u32[]{:S(2)}, u32[]{:S(2)}) collective-permute-start(f32[4,2,32,128]{3,2,1,0:T(8,128)S(1)} %get-tuple-element.18), channel_id=1, source_target_pairs={{8,16},{16,8},{9,17},{17,9},{10,18},{18,10},{11,19},{19,11},{12,20... | collective-permute-start | bytes 393224 | tf_op jit(solution)/shard_map/ppermute | solution.py:576
  17.6 4.6 %copy-start.2 = (f32[4,456,456]{2,1,0:T(8,128)S(1)}, f32[4,456,456]{2,1,0:T(8,128)}, u32[]{:S(2)}) copy-start(f32[4,456,456]{2,1,0:T(8,128)} %down_ref.1) | copy-start | bytes 9980932
  17.6 4.6 %copy-start.3 = (f32[456,456]{1,0:T(8,128)S(1)}, f32[456,456]{1,0:T(8,128)}, u32[]{:S(2)}) copy-start(f32[456,456]{1,0:T(8,128)} %inv_ref.1) | copy-start | bytes 2495236
  17.7 4.6 %copy-start.5 = (f32[12,8,456]{2,1,0:T(8,128)S(1)}, f32[12,8,456]{2,1,0:T(8,128)}, u32[]{:S(2)}) copy-start(f32[12,8,456]{2,1,0:T(8,128)} %pin_ref.1) | copy-start | bytes 525316
  17.7 4.6 %copy-start.8 = (bf16[512,456]{1,0:T(8,128)(2,1)S(1)}, bf16[512,456]{1,0:T(8,128)(2,1)}, u32[]{:S(2)}) copy-start(bf16[512,456]{1,0:T(8,128)(2,1)} %constant.33.clone.back) | copy-start | bytes 1400836

commit v2 on v1

--- a/solution.py
+++ b/solution.py
@@ -392,7 +392,8 @@
                     fresh[1, e, t // 2, 16:32, at] = x.astype(BF16)
         return carry
 
-    lax.fori_loop(0, 2, patch, 0)
+    for cs in range(2):
+        patch(cs, 0)
 
     runs = [(0, 3), (3, 6), (6, 11), (11, 16), (16, 21)]
 

time: 31.4 us -> 31.1 us (level)
  no operation moved by 1% of the time
where the time goes in v2:
time: 31.1 us; the launch traced here: 30.8 us
  Pallas kernels  14.4 us (46%)
  starting transfers between devices  7.02 us (23%)
  waiting for transfers between devices  5.12 us (16%)
  local copies, waits for them, and re-layouts  2.2 us (7%)
  other arithmetic  1.27 us (4%)
  between operations  0.79 us (3%)
    pallas_call x1, Pallas kernels, close_step(): pl.pallas_call(close_kernel, out_shape=jax.ShapeDtypeStruct(shape, F32),...  8.57 us
    ppermute x4, starting transfers between devices, swapped(): lax.ppermute(strips[kind], axis, pairs + [(j, i) for i, j in pairs])  7.02 us
    ppermute x4, waiting for transfers between devices, swapped(): lax.ppermute(strips[kind], axis, pairs + [(j, i) for i, j in pairs])  5.12 us
    pallas_call x1, Pallas kernels, near_step(): pl.pallas_call(near_kernel, out_shape=(jax.ShapeDtypeStruct(parents.shape...  2.76 us
    pallas_call x1, Pallas kernels, pass_step(): pl.pallas_call(pass_kernel, out_shape=(jax.ShapeDtypeStruct((pr, pc, dens...  2.52 us
    unnamed x20, local copies, waits for them, and re-layouts  2.2 us
    select_n x1, other arithmetic, local(): strips = (jnp.where(even[1], high, low), jnp.where(even[1], low, high))  1.2 us
  transfers between devices with their start and end apart: 4, of which 2 were waited for; matrix products, arithmetic and copies ran while one was open for 0% of the time, Pallas kernels for 11%

profile of v2, /device:TPU:19, one launch (start us, length us, event | category | flops | bytes accessed | tf_op | source)
XLA Modules:
  0.0 30.8 jit_solution(9203480934942555003)
XLA Ops:
  0.6 1.2 %slice_select_fusion = (f32[24,4,456]{2,1,0:T(4,128)S(1)}, f32[24,4,456]{2,1,0:T(4,128)S(1)}) fusion(f32[24,16,456]{2,1,0:T(8,128)} %own_ref.1, pred[]{:T(512)} %eq.10), kind=kLoop, calls=%fused_computation | loop fusion | flops 87552 | bytes 700417 | tf_op jit(solution)/shard_map/jit(_where)/select_n | solution.py:587
  1.8 3.7 %collective-permute-start.1 = (f32[24,4,456]{2,1,0:T(4,128)S(1)}, f32[24,4,456]{2,1,0:T(4,128)S(1)}, u32[]{:S(2)}, u32[]{:S(2)}) collective-permute-start(f32[24,4,456]{2,1,0:T(4,128)S(1)} %get-tuple-element.26), channel_id=1, source_target_pairs={{1,2},{3,4},{5,6},{2,1},{4,3},{6,5},{9,10},{11,12},{13,14},{10,9},... | collective-permute-start | bytes 525320 | tf_op jit(solution)/shard_map/ppermute | solution.py:577
  5.5 0.1 collective-permute-start
  5.6 0.1 add_convert_fusion.even_ref
  5.7 0.0 copy-start.1
  5.7 1.1 %copy-done.1 = f32[24,16,456]{2,1,0:T(8,128)S(1)} copy-done((f32[24,16,456]{2,1,0:T(8,128)S(1)}, f32[24,16,456]{2,1,0:T(8,128)}, u32[]{:S(2)}) %copy-start.1) | copy-done | bytes 700440
  6.8 0.0 copy-start.9
  6.8 1.0 %copy-done.9 = bf16[456,512]{1,0:T(8,128)(2,1)S(1)} copy-done((bf16[456,512]{1,0:T(8,128)(2,1)S(1)}, bf16[456,512]{1,0:T(8,128)(2,1)}, u32[]{:S(2)}) %copy-start.9) | copy-done | bytes 466968
  7.9 0.0 copy-start
  7.9 0.0 copy-start.7
  7.9 0.6 %shard_map.113 = (f32[4,24,16,128]{3,2,1,0:T(8,128)S(1)}, f32[4,24,16,128]{3,2,1,0:T(8,128)S(1)}, bf16[456,512]{1,0:T(8,128)(2,1)S(1)}) custom-call(f32[24,16,456]{2,1,0:T(8,128)S(1)} %copy-done.1, bf16[456,512]{1,0:T(8,128)(2,1)S(1)} %copy-done.9), custom_call_target="tpu_custom_call" | custom-call | flops 2415919104 | bytes 67108864 | tf_op jit(solution)/shard_map/pallas_call | solution.py:494
  8.5 0.0 copy-start.4
  8.5 0.0 copy-start.6
  8.5 3.3 %collective-permute-done.1.strip1_ref = f32[24,4,456]{2,1,0:T(4,128)S(1)} collective-permute-done((f32[24,4,456]{2,1,0:T(4,128)S(1)}, f32[24,4,456]{2,1,0:T(4,128)S(1)}, u32[]{:S(2)}, u32[]{:S(2)}) %collective-permute-start.1) | collective-permute-done | bytes 175136 | tf_op jit(solution)/shard_map/ppermute | solution.py:577
  11.8 0.0 collective-permute-done.strip0_ref
  11.8 0.0 copy-done
  11.8 2.5 %shard_map.114 = (f32[12,8,456]{2,1,0:T(8,128)S(1)}, f32[4,24,8,128]{3,2,1,0:T(8,128)S(1)}, f32[4,16,16,128]{3,2,1,0:T(8,128)S(1)}, f32[4,2,32,128]{3,2,1,0:T(8,128)S(1)}, f32[4,2,32,128]{3,2,1,0:T(8,128)S(1)}) custom-call(s32[2]{0:T(128)S(1)} %add_convert_fusion.even_ref, f32[24,4,456]{2,1,0:T(4,128)S(1)} %collective-permute-done.strip0_ref, ...), custom_call_target="tpu_custom_call" | custom-call | flops 1610612736 | bytes 3326976 | tf_op jit(solution)/shard_map/pallas_call | solution.py:509
  14.3 1.4 %collective-permute-start.2 = (f32[4,2,32,128]{3,2,1,0:T(8,128)S(1)}, f32[4,2,32,128]{3,2,1,0:T(8,128)S(1)}, u32[]{:S(2)}, u32[]{:S(2)}) collective-permute-start(f32[4,2,32,128]{3,2,1,0:T(8,128)S(1)} %get-tuple-element.17), channel_id=1, source_target_pairs={{0,8},{16,24},{8,0},{24,16},{1,9},{17,25},{9,1},{25,17},{2,10},{18... | collective-permute-start | bytes 393224 | tf_op jit(solution)/shard_map/ppermute | solution.py:577
  15.7 1.9 %collective-permute-start.3 = (f32[4,2,32,128]{3,2,1,0:T(8,128)S(1)}, f32[4,2,32,128]{3,2,1,0:T(8,128)S(1)}, u32[]{:S(2)}, u32[]{:S(2)}) collective-permute-start(f32[4,2,32,128]{3,2,1,0:T(8,128)S(1)} %get-tuple-element.18), channel_id=1, source_target_pairs={{8,16},{16,8},{9,17},{17,9},{10,18},{18,10},{11,19},{19,11},{12,20... | collective-permute-start | bytes 393224 | tf_op jit(solution)/shard_map/ppermute | solution.py:577
  17.6 0.0 copy-done.4
  17.6 0.0 copy-done.6
  17.6 0.0 copy-start.2
  17.6 0.0 copy-start.3
  17.7 0.0 copy-start.5
  17.7 0.0 copy-start.8
  17.7 2.8 %shard_map.115 = (f32[12,8,456]{2,1,0:T(8,128)}, bf16[36,2,128,256]{3,2,1,0:T(8,128)(2,1)S(1)}, bf16[108,128,128]{2,1,0:T(8,128)(2,1)S(1)}, f32[4,4,32,128]{3,2,1,0:T(8,128)S(1)}) custom-call(f32[4,24,16,128]{3,2,1,0:T(8,128)S(1)} %get-tuple-element.15.own_modes_ref, f32[4,24,8,128]{3,2,1,0:T(8,128)S(1)} %get-tuple-element.19.side_ref, ...), custom_call_target="tpu_custom_call" | custom-call | flops 2415919104 | bytes 16777216 | tf_op jit(solution)/shard_map/pallas_call | solution.py:529
  20.4 0.0 collective-permute-done.2.got0_ref
  20.4 1.8 %collective-permute-done.3.got1_ref = f32[4,2,32,128]{3,2,1,0:T(8,128)S(1)} collective-permute-done((f32[4,2,32,128]{3,2,1,0:T(8,128)S(1)}, f32[4,2,32,128]{3,2,1,0:T(8,128)S(1)}, u32[]{:S(2)}, u32[]{:S(2)}) %collective-permute-start.3) | collective-permute-done | bytes 131104 | tf_op jit(solution)/shard_map/ppermute | solution.py:577
  22.2 0.0 copy-done.7
  22.2 0.0 copy-done.2
  22.3 0.0 copy-done.3
  22.3 0.0 copy-done.5
  22.3 0.0 copy-done.8
  22.3 8.6 %shard_map.116 = f32[24,16,456]{2,1,0:T(8,128)} custom-call(s32[2]{0:T(128)S(1)} %add_convert_fusion.even_ref, f32[4,2,32,128]{3,2,1,0:T(8,128)S(1)} %collective-permute-done.2.got0_ref, f32[4,2,32,128]{3,2,1,0:T(8,128)S(1)} %collective-permute-done.3.got1_ref, f32[4,4,32,128]{3,2,1,0:T(8,128)S(1)} %get-tuple-element.22.edge_ref, ...), custom_call_target="tpu_custom_call" | custom-call | flops 7549747200 | bytes 10485760 | tf_op jit(solution)/shard_map/pallas_call | solution.py:552
Async XLA Ops:
  1.8 10.0 %collective-permute-start.1 = (f32[24,4,456]{2,1,0:T(4,128)S(1)}, f32[24,4,456]{2,1,0:T(4,128)S(1)}, u32[]{:S(2)}, u32[]{:S(2)}) collective-permute-start(f32[24,4,456]{2,1,0:T(4,128)S(1)} %get-tuple-element.26), channel_id=1, source_target_pairs={{1,2},{3,4},{5,6},{2,1},{4,3},{6,5},{9,10},{11,12},{13,14},{10,9},... | collective-permute-start | bytes 525320 | tf_op jit(solution)/shard_map/ppermute | solution.py:577
  5.5 6.3 %collective-permute-start = (f32[24,4,456]{2,1,0:T(4,128)S(1)}, f32[24,4,456]{2,1,0:T(4,128)S(1)}, u32[]{:S(2)}, u32[]{:S(2)}) collective-permute-start(f32[24,4,456]{2,1,0:T(4,128)S(1)} %get-tuple-element.27), channel_id=1, source_target_pairs={{0,1},{2,3},{4,5},{6,7},{1,0},{3,2},{5,4},{7,6},{8,9},{10,11},{12,... | collective-permute-start | bytes 525320 | tf_op jit(solution)/shard_map/ppermute | solution.py:577
  5.7 1.1 %copy-start.1 = (f32[24,16,456]{2,1,0:T(8,128)S(1)}, f32[24,16,456]{2,1,0:T(8,128)}, u32[]{:S(2)}) copy-start(f32[24,16,456]{2,1,0:T(8,128)} %own_ref.1) | copy-start | bytes 2101252
  6.8 1.0 %copy-start.9 = (bf16[456,512]{1,0:T(8,128)(2,1)S(1)}, bf16[456,512]{1,0:T(8,128)(2,1)}, u32[]{:S(2)}) copy-start(bf16[456,512]{1,0:T(8,128)(2,1)} %constant.32.clone.rot_ref) | copy-start | bytes 1400836
  7.9 3.9 %copy-start = (f32[4,456,456]{2,1,0:T(8,128)S(1)}, f32[4,456,456]{2,1,0:T(8,128)}, u32[]{:S(2)}) copy-start(f32[4,456,456]{2,1,0:T(8,128)} %up_ref.1) | copy-start | bytes 9980932
  7.9 14.4 %copy-start.7 = (bf16[2,10240,256]{2,1,0:T(8,128)(2,1)S(1)}, bf16[2,10240,256]{2,1,0:T(8,128)(2,1)}, u32[]{:S(2)}) copy-start(bf16[2,10240,256]{2,1,0:T(8,128)(2,1)} %constant.34.clone.table) | copy-start | bytes 31457284
  8.5 9.1 %copy-start.4 = (s32[24,16,40]{2,1,0:T(8,128)S(1)}, s32[24,16,40]{2,1,0:T(8,128)}, u32[]{:S(2)}) copy-start(s32[24,16,40]{2,1,0:T(8,128)} %llist_ref.1) | copy-start | bytes 184324
  8.5 9.1 %copy-start.6 = (s32[12,8,40]{2,1,0:T(8,128)S(1)}, s32[12,8,40]{2,1,0:T(8,128)}, u32[]{:S(2)}) copy-start(s32[12,8,40]{2,1,0:T(8,128)} %plist_ref.1) | copy-start | bytes 46084
  14.3 6.1 %collective-permute-start.2 = (f32[4,2,32,128]{3,2,1,0:T(8,128)S(1)}, f32[4,2,32,128]{3,2,1,0:T(8,128)S(1)}, u32[]{:S(2)}, u32[]{:S(2)}) collective-permute-start(f32[4,2,32,128]{3,2,1,0:T(8,128)S(1)} %get-tuple-element.17), channel_id=1, source_target_pairs={{0,8},{16,24},{8,0},{24,16},{1,9},{17,25},{9,1},{25,17},{2,10},{18... | collective-permute-start | bytes 393224 | tf_op jit(solution)/shard_map/ppermute | solution.py:577
  15.7 6.6 %collective-permute-start.3 = (f32[4,2,32,128]{3,2,1,0:T(8,128)S(1)}, f32[4,2,32,128]{3,2,1,0:T(8,128)S(1)}, u32[]{:S(2)}, u32[]{:S(2)}) collective-permute-start(f32[4,2,32,128]{3,2,1,0:T(8,128)S(1)} %get-tuple-element.18), channel_id=1, source_target_pairs={{8,16},{16,8},{9,17},{17,9},{10,18},{18,10},{11,19},{19,11},{12,20... | collective-permute-start | bytes 393224 | tf_op jit(solution)/shard_map/ppermute | solution.py:577
  17.6 4.6 %copy-start.2 = (f32[4,456,456]{2,1,0:T(8,128)S(1)}, f32[4,456,456]{2,1,0:T(8,128)}, u32[]{:S(2)}) copy-start(f32[4,456,456]{2,1,0:T(8,128)} %down_ref.1) | copy-start | bytes 9980932
  17.6 4.6 %copy-start.3 = (f32[456,456]{1,0:T(8,128)S(1)}, f32[456,456]{1,0:T(8,128)}, u32[]{:S(2)}) copy-start(f32[456,456]{1,0:T(8,128)} %inv_ref.1) | copy-start | bytes 2495236
  17.7 4.6 %copy-start.5 = (f32[12,8,456]{2,1,0:T(8,128)S(1)}, f32[12,8,456]{2,1,0:T(8,128)}, u32[]{:S(2)}) copy-start(f32[12,8,456]{2,1,0:T(8,128)} %pin_ref.1) | copy-start | bytes 525316
  17.7 4.6 %copy-start.8 = (bf16[512,456]{1,0:T(8,128)(2,1)S(1)}, bf16[512,456]{1,0:T(8,128)(2,1)}, u32[]{:S(2)}) copy-start(bf16[512,456]{1,0:T(8,128)(2,1)} %constant.33.clone.back) | copy-start | bytes 1400836

commit v3 on v2

--- a/solution.py
+++ b/solution.py
@@ -348,7 +348,7 @@
     got0_ref, got1_ref, edge_ref, pside_ref, masks, lut,
     pin_ref, back, table, down_ref, inv_ref,
     out_ref,
-    edge, pmodes, fresh, acc, flat, plocal,
+    edge, pmodes, fresh, flat, plocal,
 ):
     rows, cols, dens = out_ref.shape
     pr, pc = rows // 2, cols // 2
@@ -412,9 +412,10 @@
             x = jnp.concatenate(pieces, axis=0)
         return jnp.concatenate([x[:, :128] * m, x[:, 128:] * m], axis=1)
 
+    checks, pchecks = [], []
     for c in range(2):
 
-        def interact(s, carry):
+        def interact(s):
             n = 2 * c
             total = jnp.zeros((2 * high, 256), F32)
 
@@ -427,37 +428,29 @@
                 x, weight = run(n * count + a, n * count + b, s)
                 y, _ = run((n + 1) * count + a, (n + 1) * count + b, s)
                 total = total + dot(jnp.concatenate([x, y], axis=0), weight)
+            ends = []
             for d in range(2):
                 x, weight = run((n + d) * count + runs[-1][1], (n + d + 1) * count, s)
-                acc[s, n + d] = total[high * d : high * (d + 1)] + dot(x, weight)
-            return carry
-
-        for s in range(2):
-            interact(s, 0)
-
-    def densities(rows):
-        pieces = [
-            times_exact(
-                jnp.concatenate([acc[s, n, rows] for n in range(4)], axis=0),
-                back[256 * s : 256 * (s + 1)],
-            )
-            for s in range(2)
-        ]
-        return pieces[0] + pieces[1]
-
-    pcheck = densities(slice(boxes, high))
-    check = densities(slice(0, boxes))
+                ends.append(dot(x, weight))
+            return total + jnp.concatenate(ends, axis=0)
+
+        mapped = [times_exact(interact(s), back[256 * s : 256 * (s + 1)]) for s in range(2)]
+        mapped = mapped[0] + mapped[1]
+        for d in range(2):
+            checks.append(mapped[high * d : high * d + boxes])
+            pchecks.append(mapped[high * d + boxes : high * (d + 1)])
 
     inverse = parts(inv_ref[...])
     for n, (c, d) in enumerate(class_pairs()):
         for t, cut, to in cut_tiles(dens):
             for j in range(gr):
-                r = (high - boxes) * n + gc * j
-                plocal[t, 2 * j + c, pl.ds(d, gc, stride=2), to] = pcheck[r : r + gc, cut]
+                plocal[t, 2 * j + c, pl.ds(d, gc, stride=2), to] = pchecks[n][
+                    gc * j : gc * (j + 1), cut
+                ]
     local = pin_ref[...].reshape(boxes, dens) + times_t(lanes(plocal)[:, :dens], inverse)
     x = jnp.concatenate(
         [
-            check[boxes * n : boxes * (n + 1)] + times_t(local, parts(down_ref[n]))
+            checks[n] + times_t(local, parts(down_ref[n]))
             for n in range(4)
         ],
         axis=0,
@@ -558,7 +551,6 @@
             pltpu.VMEM((4, 8, cols + 16, 128), F32),
             pltpu.VMEM((4, pr + 4, pc + 8, 128), F32),
             pltpu.VMEM((2, 12, 2, 32, 256), BF16),
-            pltpu.VMEM((2, 4, high, 256), F32),
             pltpu.VMEM((4, rows, cols, 128), F32),
             pltpu.VMEM((4, pr, pc, 128), F32),
         ],

time: 31.1 us -> 34.8 us (1.12)
  Pallas kernels: 14.4 us -> 18.2 us
    pallas_call x1, Pallas kernels: 8.57 us -> 12.3 us  [close_step(): pl.pallas_call(close_kernel, out_shape=jax.ShapeDtypeStruct(shape, F32),...]
  transfers between devices with their start and end apart: 4 -> 4, of which waited for: 2 -> 2; matrix products, arithmetic and copies ran while one was open for 0% -> 0% of each run, Pallas kernels for 11% -> 10%
where the time goes in v3:
time: 34.8 us; the launch traced here: 34.6 us
  Pallas kernels  18.2 us (52%)
  starting transfers between devices  7.02 us (20%)
  waiting for transfers between devices  5.12 us (15%)
  local copies, waits for them, and re-layouts  2.2 us (6%)
  other arithmetic  1.27 us (4%)
  between operations  0.79 us (2%)
    pallas_call x1, Pallas kernels, close_step(): pl.pallas_call(close_kernel, out_shape=jax.ShapeDtypeStruct(shape, F32),...  12.3 us
    ppermute x4, starting transfers between devices, swapped(): lax.ppermute(strips[kind], axis, pairs + [(j, i) for i, j in pairs])  7.02 us
    ppermute x4, waiting for transfers between devices, swapped(): lax.ppermute(strips[kind], axis, pairs + [(j, i) for i, j in pairs])  5.12 us
    pallas_call x1, Pallas kernels, near_step(): pl.pallas_call(near_kernel, out_shape=(jax.ShapeDtypeStruct(parents.shape...  2.76 us
    pallas_call x1, Pallas kernels, pass_step(): pl.pallas_call(pass_kernel, out_shape=(jax.ShapeDtypeStruct((pr, pc, dens...  2.52 us
    unnamed x20, local copies, waits for them, and re-layouts  2.2 us
    select_n x1, other arithmetic, local(): strips = (jnp.where(even[1], high, low), jnp.where(even[1], low, high))  1.2 us
  transfers between devices with their start and end apart: 4, of which 2 were waited for; matrix products, arithmetic and copies ran while one was open for 0% of the time, Pallas kernels for 10%

profile of v3, /device:TPU:19, one launch (start us, length us, event | category | flops | bytes accessed | tf_op | source)
XLA Modules:
  0.0 34.6 jit_solution(7095713868800840915)
XLA Ops:
  0.6 1.2 %slice_select_fusion = (f32[24,4,456]{2,1,0:T(4,128)S(1)}, f32[24,4,456]{2,1,0:T(4,128)S(1)}) fusion(f32[24,16,456]{2,1,0:T(8,128)} %own_ref.1, pred[]{:T(512)} %eq.10), kind=kLoop, calls=%fused_computation | loop fusion | flops 87552 | bytes 700417 | tf_op jit(solution)/shard_map/jit(_where)/select_n | solution.py:579
  1.8 3.7 %collective-permute-start.1 = (f32[24,4,456]{2,1,0:T(4,128)S(1)}, f32[24,4,456]{2,1,0:T(4,128)S(1)}, u32[]{:S(2)}, u32[]{:S(2)}) collective-permute-start(f32[24,4,456]{2,1,0:T(4,128)S(1)} %get-tuple-element.26), channel_id=1, source_target_pairs={{1,2},{3,4},{5,6},{2,1},{4,3},{6,5},{9,10},{11,12},{13,14},{10,9},... | collective-permute-start | bytes 525320 | tf_op jit(solution)/shard_map/ppermute | solution.py:569
  5.5 0.1 collective-permute-start
  5.6 0.1 add_convert_fusion.even_ref
  5.7 0.0 copy-start.1
  5.7 1.1 %copy-done.1 = f32[24,16,456]{2,1,0:T(8,128)S(1)} copy-done((f32[24,16,456]{2,1,0:T(8,128)S(1)}, f32[24,16,456]{2,1,0:T(8,128)}, u32[]{:S(2)}) %copy-start.1) | copy-done | bytes 700440
  6.8 0.0 copy-start.9
  6.8 1.0 %copy-done.9 = bf16[456,512]{1,0:T(8,128)(2,1)S(1)} copy-done((bf16[456,512]{1,0:T(8,128)(2,1)S(1)}, bf16[456,512]{1,0:T(8,128)(2,1)}, u32[]{:S(2)}) %copy-start.9) | copy-done | bytes 466968
  7.9 0.0 copy-start
  7.9 0.0 copy-start.7
  7.9 0.6 %shard_map.113 = (f32[4,24,16,128]{3,2,1,0:T(8,128)S(1)}, f32[4,24,16,128]{3,2,1,0:T(8,128)S(1)}, bf16[456,512]{1,0:T(8,128)(2,1)S(1)}) custom-call(f32[24,16,456]{2,1,0:T(8,128)S(1)} %copy-done.1, bf16[456,512]{1,0:T(8,128)(2,1)S(1)} %copy-done.9), custom_call_target="tpu_custom_call" | custom-call | flops 2415919104 | bytes 67108864 | tf_op jit(solution)/shard_map/pallas_call | solution.py:487
  8.5 0.0 copy-start.4
  8.5 0.0 copy-start.6
  8.5 3.3 %collective-permute-done.1.strip1_ref = f32[24,4,456]{2,1,0:T(4,128)S(1)} collective-permute-done((f32[24,4,456]{2,1,0:T(4,128)S(1)}, f32[24,4,456]{2,1,0:T(4,128)S(1)}, u32[]{:S(2)}, u32[]{:S(2)}) %collective-permute-start.1) | collective-permute-done | bytes 175136 | tf_op jit(solution)/shard_map/ppermute | solution.py:569
  11.8 0.0 collective-permute-done.strip0_ref
  11.8 0.0 copy-done
  11.8 2.5 %shard_map.114 = (f32[12,8,456]{2,1,0:T(8,128)S(1)}, f32[4,24,8,128]{3,2,1,0:T(8,128)S(1)}, f32[4,16,16,128]{3,2,1,0:T(8,128)S(1)}, f32[4,2,32,128]{3,2,1,0:T(8,128)S(1)}, f32[4,2,32,128]{3,2,1,0:T(8,128)S(1)}) custom-call(s32[2]{0:T(128)S(1)} %add_convert_fusion.even_ref, f32[24,4,456]{2,1,0:T(4,128)S(1)} %collective-permute-done.strip0_ref, ...), custom_call_target="tpu_custom_call" | custom-call | flops 1610612736 | bytes 3326976 | tf_op jit(solution)/shard_map/pallas_call | solution.py:502
  14.3 1.4 %collective-permute-start.2 = (f32[4,2,32,128]{3,2,1,0:T(8,128)S(1)}, f32[4,2,32,128]{3,2,1,0:T(8,128)S(1)}, u32[]{:S(2)}, u32[]{:S(2)}) collective-permute-start(f32[4,2,32,128]{3,2,1,0:T(8,128)S(1)} %get-tuple-element.17), channel_id=1, source_target_pairs={{0,8},{16,24},{8,0},{24,16},{1,9},{17,25},{9,1},{25,17},{2,10},{18... | collective-permute-start | bytes 393224 | tf_op jit(solution)/shard_map/ppermute | solution.py:569
  15.7 1.9 %collective-permute-start.3 = (f32[4,2,32,128]{3,2,1,0:T(8,128)S(1)}, f32[4,2,32,128]{3,2,1,0:T(8,128)S(1)}, u32[]{:S(2)}, u32[]{:S(2)}) collective-permute-start(f32[4,2,32,128]{3,2,1,0:T(8,128)S(1)} %get-tuple-element.18), channel_id=1, source_target_pairs={{8,16},{16,8},{9,17},{17,9},{10,18},{18,10},{11,19},{19,11},{12,20... | collective-permute-start | bytes 393224 | tf_op jit(solution)/shard_map/ppermute | solution.py:569
  17.6 0.0 copy-done.4
  17.6 0.0 copy-done.6
  17.6 0.0 copy-start.2
  17.6 0.0 copy-start.3
  17.7 0.0 copy-start.5
  17.7 0.0 copy-start.8
  17.7 2.8 %shard_map.115 = (f32[12,8,456]{2,1,0:T(8,128)}, bf16[36,2,128,256]{3,2,1,0:T(8,128)(2,1)S(1)}, bf16[108,128,128]{2,1,0:T(8,128)(2,1)S(1)}, f32[4,4,32,128]{3,2,1,0:T(8,128)S(1)}) custom-call(f32[4,24,16,128]{3,2,1,0:T(8,128)S(1)} %get-tuple-element.15.own_modes_ref, f32[4,24,8,128]{3,2,1,0:T(8,128)S(1)} %get-tuple-element.19.side_ref, ...), custom_call_target="tpu_custom_call" | custom-call | flops 2415919104 | bytes 16777216 | tf_op jit(solution)/shard_map/pallas_call | solution.py:522
  20.4 0.0 collective-permute-done.2.got0_ref
  20.4 1.8 %collective-permute-done.3.got1_ref = f32[4,2,32,128]{3,2,1,0:T(8,128)S(1)} collective-permute-done((f32[4,2,32,128]{3,2,1,0:T(8,128)S(1)}, f32[4,2,32,128]{3,2,1,0:T(8,128)S(1)}, u32[]{:S(2)}, u32[]{:S(2)}) %collective-permute-start.3) | collective-permute-done | bytes 131104 | tf_op jit(solution)/shard_map/ppermute | solution.py:569
  22.2 0.0 copy-done.7
  22.2 0.0 copy-done.2
  22.3 0.0 copy-done.3
  22.3 0.0 copy-done.5
  22.3 0.0 copy-done.8
  22.3 12.3 %shard_map.116 = f32[24,16,456]{2,1,0:T(8,128)} custom-call(s32[2]{0:T(128)S(1)} %add_convert_fusion.even_ref, f32[4,2,32,128]{3,2,1,0:T(8,128)S(1)} %collective-permute-done.2.got0_ref, f32[4,2,32,128]{3,2,1,0:T(8,128)S(1)} %collective-permute-done.3.got1_ref, f32[4,4,32,128]{3,2,1,0:T(8,128)S(1)} %get-tuple-element.22.edge_ref, ...), custom_call_target="tpu_custom_call" | custom-call | flops 7549747200 | bytes 10485760 | tf_op jit(solution)/shard_map/pallas_call | solution.py:545
Async XLA Ops:
  1.8 10.0 %collective-permute-start.1 = (f32[24,4,456]{2,1,0:T(4,128)S(1)}, f32[24,4,456]{2,1,0:T(4,128)S(1)}, u32[]{:S(2)}, u32[]{:S(2)}) collective-permute-start(f32[24,4,456]{2,1,0:T(4,128)S(1)} %get-tuple-element.26), channel_id=1, source_target_pairs={{1,2},{3,4},{5,6},{2,1},{4,3},{6,5},{9,10},{11,12},{13,14},{10,9},... | collective-permute-start | bytes 525320 | tf_op jit(solution)/shard_map/ppermute | solution.py:569
  5.5 6.3 %collective-permute-start = (f32[24,4,456]{2,1,0:T(4,128)S(1)}, f32[24,4,456]{2,1,0:T(4,128)S(1)}, u32[]{:S(2)}, u32[]{:S(2)}) collective-permute-start(f32[24,4,456]{2,1,0:T(4,128)S(1)} %get-tuple-element.27), channel_id=1, source_target_pairs={{0,1},{2,3},{4,5},{6,7},{1,0},{3,2},{5,4},{7,6},{8,9},{10,11},{12,... | collective-permute-start | bytes 525320 | tf_op jit(solution)/shard_map/ppermute | solution.py:569
  5.7 1.1 %copy-start.1 = (f32[24,16,456]{2,1,0:T(8,128)S(1)}, f32[24,16,456]{2,1,0:T(8,128)}, u32[]{:S(2)}) copy-start(f32[24,16,456]{2,1,0:T(8,128)} %own_ref.1) | copy-start | bytes 2101252
  6.8 1.0 %copy-start.9 = (bf16[456,512]{1,0:T(8,128)(2,1)S(1)}, bf16[456,512]{1,0:T(8,128)(2,1)}, u32[]{:S(2)}) copy-start(bf16[456,512]{1,0:T(8,128)(2,1)} %constant.32.clone.rot_ref) | copy-start | bytes 1400836
  7.9 3.9 %copy-start = (f32[4,456,456]{2,1,0:T(8,128)S(1)}, f32[4,456,456]{2,1,0:T(8,128)}, u32[]{:S(2)}) copy-start(f32[4,456,456]{2,1,0:T(8,128)} %up_ref.1) | copy-start | bytes 9980932
  7.9 14.4 %copy-start.7 = (bf16[2,10240,256]{2,1,0:T(8,128)(2,1)S(1)}, bf16[2,10240,256]{2,1,0:T(8,128)(2,1)}, u32[]{:S(2)}) copy-start(bf16[2,10240,256]{2,1,0:T(8,128)(2,1)} %constant.34.clone.table) | copy-start | bytes 31457284
  8.5 9.1 %copy-start.4 = (s32[24,16,40]{2,1,0:T(8,128)S(1)}, s32[24,16,40]{2,1,0:T(8,128)}, u32[]{:S(2)}) copy-start(s32[24,16,40]{2,1,0:T(8,128)} %llist_ref.1) | copy-start | bytes 184324
  8.5 9.1 %copy-start.6 = (s32[12,8,40]{2,1,0:T(8,128)S(1)}, s32[12,8,40]{2,1,0:T(8,128)}, u32[]{:S(2)}) copy-start(s32[12,8,40]{2,1,0:T(8,128)} %plist_ref.1) | copy-start | bytes 46084
  14.3 6.1 %collective-permute-start.2 = (f32[4,2,32,128]{3,2,1,0:T(8,128)S(1)}, f32[4,2,32,128]{3,2,1,0:T(8,128)S(1)}, u32[]{:S(2)}, u32[]{:S(2)}) collective-permute-start(f32[4,2,32,128]{3,2,1,0:T(8,128)S(1)} %get-tuple-element.17), channel_id=1, source_target_pairs={{0,8},{16,24},{8,0},{24,16},{1,9},{17,25},{9,1},{25,17},{2,10},{18... | collective-permute-start | bytes 393224 | tf_op jit(solution)/shard_map/ppermute | solution.py:569
  15.7 6.6 %collective-permute-start.3 = (f32[4,2,32,128]{3,2,1,0:T(8,128)S(1)}, f32[4,2,32,128]{3,2,1,0:T(8,128)S(1)}, u32[]{:S(2)}, u32[]{:S(2)}) collective-permute-start(f32[4,2,32,128]{3,2,1,0:T(8,128)S(1)} %get-tuple-element.18), channel_id=1, source_target_pairs={{8,16},{16,8},{9,17},{17,9},{10,18},{18,10},{11,19},{19,11},{12,20... | collective-permute-start | bytes 393224 | tf_op jit(solution)/shard_map/ppermute | solution.py:569
  17.6 4.6 %copy-start.2 = (f32[4,456,456]{2,1,0:T(8,128)S(1)}, f32[4,456,456]{2,1,0:T(8,128)}, u32[]{:S(2)}) copy-start(f32[4,456,456]{2,1,0:T(8,128)} %down_ref.1) | copy-start | bytes 9980932
  17.6 4.6 %copy-start.3 = (f32[456,456]{1,0:T(8,128)S(1)}, f32[456,456]{1,0:T(8,128)}, u32[]{:S(2)}) copy-start(f32[456,456]{1,0:T(8,128)} %inv_ref.1) | copy-start | bytes 2495236
  17.7 4.6 %copy-start.5 = (f32[12,8,456]{2,1,0:T(8,128)S(1)}, f32[12,8,456]{2,1,0:T(8,128)}, u32[]{:S(2)}) copy-start(f32[12,8,456]{2,1,0:T(8,128)} %pin_ref.1) | copy-start | bytes 525316
  17.7 4.6 %copy-start.8 = (bf16[512,456]{1,0:T(8,128)(2,1)S(1)}, bf16[512,456]{1,0:T(8,128)(2,1)}, u32[]{:S(2)}) copy-start(bf16[512,456]{1,0:T(8,128)(2,1)} %constant.33.clone.back) | copy-start | bytes 1400836
